TPU v7x, 256 devices: a whole 4x4x8 slice. The times are simulated.
256 devices in a mesh: seq: 16 (over z, core), wt: 16 (over x, y).
Axes of the slice: x: 4, y: 4, z: 8, core: 2. Of those that a mesh axis runs over, the one named last changes fastest.
Arguments:
- queries: bfloat16 [8192, 8192], P('seq', 'wt'), may hold values from -6 to 6
- keys_in: bfloat16 [8192, 8192], P('seq', 'wt'), may hold values from -6 to 6
- values_in: bfloat16 [8192, 8192], P('seq', 'wt'), may hold values from -6 to 6
- stream: bfloat16 [8192, 8192], P('seq', 'wt')
- attn_gain: float32 [8192], P('wt'), may hold values from 0.1 to 1.9
- mlp_gain: float32 [8192], replicated, may hold values from 0.1 to 1.9
- up_index: int32 [128, 16], P('wt'), may hold values from 0 to 63, all different within a row
- up_blocks: bfloat16 [128, 16, 128, 128], P('wt'), may hold values from -0.125 to 0.125
- down_index: int32 [128, 16], P('wt'), may hold values from 0 to 63, all different within a row
- down_blocks: bfloat16 [128, 16, 128, 128], P('wt'), may hold values from -0.09375 to 0.09375
Outputs:
- result: bfloat16 [8192, 8192], P('seq', 'wt')
Inputs may be any that keep to these rules, and one draw needn't show every extreme that they name: `up_index`: each row names 16 different feature blocks, and every feature block is named by some row. `down_index`: each row names 16 different output blocks, and every output block is named by some row.
All inputs are finite; a program needn't handle non-finite values.
Results may differ from a plain program's by a relative error of at most 0.013.
Values may be sent and summed in bfloat16 or wider, within the bound.
No kernel may reach another device: no remote copies, remote signals or barrier semaphores. Data moves between devices by JAX's collectives and lax.ppermute only.
A program may use at most 128 MiB of HBM per device.

v0:
```python
import jax
import jax.numpy as jnp
from jax import lax
from jax.sharding import PartitionSpec as P

HEAD = 128
BLK = 128


def carried_in(x, axis, join, neutral):
    place = lax.axis_index(axis)
    gathered = lax.all_gather(x.astype(jnp.bfloat16), axis)
    state = jnp.zeros_like(x) + jnp.asarray(neutral, x.dtype)

    def one(step, state):
        return join(state, lax.dynamic_index_in_dim(gathered, step, 0, False).astype(x.dtype))

    return lax.fori_loop(0, place, one, state)


def feature_map(a):
    return (jax.nn.elu(a.astype(jnp.float32)) + 1.0).astype(jnp.bfloat16)


def add_states(earlier, later):
    return earlier + later


def per_device(
    queries,
    keys_in,
    values_in,
    stream,
    attn_gain,
    mlp_gain,
    up_index,
    up_blocks,
    down_index,
    down_blocks,
):
    rows = queries.shape[0]
    local_cols = queries.shape[1]
    local_heads = local_cols // HEAD
    fq = feature_map(queries).reshape(rows, local_heads, HEAD)
    fk = feature_map(keys_in).reshape(rows, local_heads, HEAD)
    vals = values_in.reshape(rows, local_heads, HEAD)
    causal = jnp.tril(jnp.ones((rows, rows), dtype=bool))
    scores = jnp.einsum("thd,shd->hts", fq, fk, preferred_element_type=jnp.float32)
    scores = jnp.where(causal[None], scores, 0.0).astype(jnp.bfloat16)
    intra = jnp.einsum("hts,shd->thd", scores, vals, preferred_element_type=jnp.float32)
    own_state = jnp.einsum("shd,she->hde", fk, vals, preferred_element_type=jnp.float32)
    empty = jnp.zeros_like(own_state)
    before = carried_in(own_state, "seq", add_states, empty)
    inter = jnp.einsum(
        "thd,hde->the", fq.astype(jnp.float32), before, precision=lax.Precision.HIGHEST
    )
    raw = intra + inter
    normal_raw = raw * lax.rsqrt(jnp.mean(raw * raw, axis=-1, keepdims=True) + 1e-06)
    attn = normal_raw.reshape(rows, local_cols) * attn_gain
    mid = (stream.astype(jnp.float32) + attn).astype(jnp.bfloat16)
    width = mlp_gain.shape[0]
    whole = lax.all_gather(mid, "wt", axis=1, tiled=True)
    whole_f = whole.astype(jnp.float32)
    scale = lax.rsqrt(jnp.mean(whole_f * whole_f, axis=-1, keepdims=True) + 1e-06)
    normed = (whole_f * scale * mlp_gain).astype(jnp.bfloat16)
    tiles = normed.reshape(rows, width // BLK, BLK)
    own_blocks = up_blocks.shape[0]
    picks = jnp.take(tiles, up_index.reshape(-1), axis=1)
    picks = picks.reshape(rows, own_blocks, up_index.shape[1], BLK)
    upper = jnp.einsum("lckd,ckde->lce", picks, up_blocks, preferred_element_type=jnp.float32)
    act = jax.nn.silu(upper).astype(jnp.bfloat16)
    parts = jnp.einsum("lrd,rkde->rkle", act, down_blocks, preferred_element_type=jnp.float32)
    parts = parts.reshape(-1, rows, BLK)
    summed = jax.ops.segment_sum(parts, down_index.reshape(-1), num_segments=width // BLK)
    partial_sum = summed.astype(jnp.bfloat16)
    mine = lax.psum_scatter(partial_sum, "wt", scatter_dimension=0, tiled=True).astype(jnp.float32)
    down = jnp.transpose(mine, (1, 0, 2)).reshape(rows, local_cols)
    return (mid.astype(jnp.float32) + down).astype(jnp.bfloat16)


def solution(mesh):
    placed = (
        P("seq", "wt"),
        P("seq", "wt"),
        P("seq", "wt"),
        P("seq", "wt"),
        P("wt"),
        P(),
        P("wt", None),
        P("wt", None, None, None),
        P("wt", None),
        P("wt", None, None, None),
    )
    return jax.shard_map(
        per_device, mesh=mesh, in_specs=placed, out_specs=P("seq", "wt"), check_vma=False
    )
```

profile of v0, /device:TPU:2, one launch (start us, length us, event | category | flops | bytes accessed | tf_op | source)
XLA Modules:
  0.0 391.9 jit_solution(10710767317259980740)
XLA Ops:
  6.5 0.0 copy-start
  6.5 0.0 copy-start.8
  6.5 0.0 all-gather.6.cloned.1.call-start
  6.5 1.6 fusion.27
  8.1 0.2 copy.49
  8.4 0.0 copy-done
  8.4 0.9 convolution_convert_fusion
  9.3 0.0 all-gather.6.cloned.1.call-update
  9.3 0.0 all-gather.4.cloned.1.call-start
  9.4 1.3 copy.35
  10.6 0.0 copy-start.7
  10.7 0.1 iota_compare_fusion
  10.7 41.4 %all-gather.6.cloned.1.call-done = bf16[64,128,128]{2,1,0:T(8,128)(2,1)} async-done(((bf16[4,128,128]{2,1,0:T(8,128)(2,1)}), bf16[64,128,128]{2,1,0:T(8,128)(2,1)}) %all-gather.6.cloned.1.call-update) | async-done | bytes 2097168 | tf_op jit(solution)/shard_map/all_gather | solution.py:12
  52.2 0.0 copy-start.6
  52.2 0.0 copy-start.5
  52.2 0.0 copy-done.8
  52.2 1.9 convolution_bitcast_fusion
  54.2 2.8 multiply_reduce_fusion
  57.0 0.0 copy-start.4
  57.1 0.1 broadcast_multiply_fusion
  57.2 0.0 copy-done.7
  57.2 1.0 fusion.30
  58.2 0.0 all-gather.4.cloned.1.call-update
  58.2 0.2 reduce-scatter.2.cloned.1.call-start
  58.5 0.0 copy-done.6
  58.5 0.1 reshape.114
  58.6 0.0 copy-done.5
  58.6 0.1 reshape.96
  58.7 87.3 %all-gather.4.cloned.1.call-done = bf16[512,8192]{0,1:T(8,128)(2,1)} async-done(((bf16[512,512]{0,1:T(8,128)(2,1)}), bf16[512,8192]{0,1:T(8,128)(2,1)}) %all-gather.4.cloned.1.call-update) | async-done | bytes 8388624 | tf_op jit(solution)/shard_map/all_gather | solution.py:62
  146.0 0.0 copy-start.2
  146.0 5.3 %fusion = f32[512]{0:T(512)S(1)} fusion(bf16[512,8192]{0,1:T(8,128)(2,1)} %all-gather.4.cloned.1.call-done), kind=kLoop, calls=%fused_computation.5 | loop fusion | flops 12582400 | bytes 8390656 | tf_op jit(solution)/shard_map/reduce_sum | solution.py:64
  151.3 0.0 copy-done.4
  151.3 0.4 copy-done.2
  151.7 4.4 %fusion.2 = bf16[512,8192]{0,1:T(8,128)(2,1)} fusion(bf16[512,8192]{0,1:T(8,128)(2,1)S(1)} %copy-done.2, f32[8192]{0:T(1024)S(1)} %copy-done.4, f32[512]{0:T(512)S(1)} %add_rsqrt_fusion.1), kind=kLoop, calls=%fused_computation.7 | loop fusion | flops 16777216 | bytes 16812032 | tf_op jit(solution)/shard_map/convert_element_type | solution.py:65
  156.1 12.0 %copy.43 = bf16[512,64,128]{2,0,1:T(8,128)(2,1)} copy(bf16[512,64,128]{0,2,1:T(8,128)(2,1)} %bitcast.96) | data formatting | bytes 16777216 | tf_op jit(solution)/shard_map/reshape | solution.py:66
  168.1 11.8 %gather_fusion = bf16[128,512,128]{2,1,0:T(8,128)(2,1)} fusion(bf16[512,64,128]{2,0,1:T(8,128)(2,1)} %copy.43, s32[1024]{0:T(1024)S(1)} %pad_clamp_fusion), kind=kCustom, calls=%fused_computation | custom fusion | bytes 33554944 | tf_op jit(solution)/shard_map/jit(_take)/gather | solution.py:68
  179.9 21.8 %fusion.20 = f32[8,512,16,128]{3,1,2,0:T(8,128)} fusion(bf16[8,16,128,128]{3,2,1,0:T(8,128)(2,1)} %param.21, bf16[8,16,128,128]{3,2,1,0:T(8,128)(2,1)} %param.19, bf16[512,8,16,128]{3,0,2,1:T(8,128)(2,1)} %bitcast.95, pred[8,16]{1,0:T(8,128)(4,1)S(1)} %compare_and_fusion), kind=kOutput, calls=%fused_computation.28 | convolution fusion | flops 4305977344 | bytes 58720384 | tf_op jit(solution)/shard_map/lrd,rkde->rkle/dot_general | solution.py:72
  201.7 7.8 %broadcast_in_dim.43 = f32[64,512,128]{2,1,0:T(8,128)} broadcast(f32[]{:T(128)} %constant.27.clone.1), dimensions={} | broadcast | bytes 16777220 | tf_op jit(solution)/shard_map/broadcast_in_dim | solution.py:74
  209.5 73.8 %scatter_fusion = f32[64,512,128]{2,1,0:T(8,128)} fusion(f32[64,512,128]{2,1,0:T(8,128)} %broadcast_in_dim.43, s32[128]{0:T(128)S(1)} %reshape.114, f32[128,512,128]{2,1,0:T(8,128)} %bitcast.94), kind=kCustom, calls=%fused_computation.1 | custom fusion | flops 8388608 | bytes 100663808 | tf_op jit(solution)/shard_map/scatter-add | solution.py:74
  283.3 9.3 %convert_element_type.62 = bf16[64,512,128]{2,1,0:T(8,128)(2,1)} convert(f32[64,512,128]{2,1,0:T(8,128)} %scatter_fusion) | non-fusion elementwise | flops 4194304 | bytes 25165824 | tf_op jit(solution)/shard_map/convert_element_type | solution.py:75
  292.6 0.0 reduce-scatter.2.cloned.1.call-update
  292.6 90.1 %reduce-scatter.2.cloned.1.call-done = bf16[4,512,128]{2,1,0:T(8,128)(2,1)} async-done(((bf16[64,512,128]{2,1,0:T(8,128)(2,1)}), bf16[4,512,128]{2,1,0:T(8,128)(2,1)}) %reduce-scatter.2.cloned.1.call-update) | async-done | bytes 524304 | tf_op jit(solution)/shard_map/reduce_scatter | solution.py:76
  382.7 1.1 convert_bitcast_fusion
  383.8 0.3 copy.44
  384.2 0.0 copy-done.3
  384.2 0.2 fusion.28
  384.4 1.0 copy.45
  385.4 0.0 copy-done.1
  (9 shorter events, 0.1 us)
Async XLA Ops:
  6.5 1.8 copy-start
  6.5 45.7 %copy-start.8 = (bf16[512,512]{1,0:T(8,128)(2,1)S(1)}, bf16[512,512]{1,0:T(8,128)(2,1)}, u32[]{:S(2)}) copy-start(bf16[512,512]{1,0:T(8,128)(2,1)} %param.12) | copy-start | bytes 1572868
  6.5 45.6 %all-gather.6.cloned.1.call-start = ((), (), s32[]{:S(2)}) async-start(), calls=%async_computation.3 | async-start | bytes 2228224 | tf_op jit(solution)/shard_map/all_gather | solution.py:12
  9.3 136.6 %all-gather.4.cloned.1.call-start = ((), (), s32[]{:S(2)}) async-start(), calls=%async_computation.1 | async-start | bytes 8912896 | tf_op jit(solution)/shard_map/all_gather | solution.py:62
  10.6 46.6 %copy-start.7 = (f32[512]{0:T(512)S(1)}, f32[512]{0:T(512)}, u32[]{:S(2)}) copy-start(f32[512]{0:T(512)} %param.16) | copy-start | bytes 6148
  52.2 6.3 %copy-start.6 = (s32[8,16]{1,0:T(8,128)S(1)}, s32[8,16]{1,0:T(8,128)}, u32[]{:S(2)}) copy-start(s32[8,16]{1,0:T(8,128)} %param.20) | copy-start | bytes 1540
  52.2 6.3 %copy-start.5 = (s32[8,16]{1,0:T(8,128)S(1)}, s32[8,16]{1,0:T(8,128)}, u32[]{:S(2)}) copy-start(s32[8,16]{1,0:T(8,128)} %param.18) | copy-start | bytes 1540
  57.0 94.2 %copy-start.4 = (f32[8192]{0:T(1024)S(1)}, f32[8192]{0:T(1024)}, u32[]{:S(2)}) copy-start(f32[8192]{0:T(1024)} %param.17) | copy-start | bytes 98308
  58.2 324.5 %reduce-scatter.2.cloned.1.call-start = ((), (), s32[]{:S(2)}) async-start(), calls=%async_computation.2 | async-start | bytes 8912896 | tf_op jit(solution)/shard_map/reduce_scatter | solution.py:76
  146.0 5.8 %copy-start.2 = (bf16[512,8192]{0,1:T(8,128)(2,1)S(1)}, bf16[512,8192]{0,1:T(8,128)(2,1)}, u32[]{:S(2)}) copy-start(bf16[512,8192]{0,1:T(8,128)(2,1)} %all-gather.4.cloned.1.call-done) | copy-start | bytes 25165828
  283.3 102.1 %copy-start.1 = (bf16[512,512]{1,0:T(8,128)(2,1)S(1)}, bf16[512,512]{1,0:T(8,128)(2,1)}, u32[]{:S(2)}) copy-start(bf16[512,512]{1,0:T(8,128)(2,1)} %param.14) | copy-start | bytes 1572868
  292.6 91.6 %copy-start.3 = (bf16[512,512]{0,1:T(8,128)(2,1)S(1)}, bf16[512,512]{0,1:T(8,128)(2,1)}, u32[]{:S(2)}) copy-start(bf16[512,512]{0,1:T(8,128)(2,1)} %fusion.30) | copy-start | bytes 1572868
Sparse Core Ops, SparseCore 0:
  9.5 42.6 all-gather.5
  58.4 87.5 all-gather.3
  292.7 89.9 reduce-scatter.1
where the time goes:
time: 393 us; the launch traced here: 392 us
  waiting for transfers between devices  219 us (56%)
  other arithmetic  96.8 us (25%)
  local copies, waits for them, and re-layouts  35.1 us (9%)
  matrix products  27.6 us (7%)
  between operations  13.3 us (3%)
    reduce_scatter x1, waiting for transfers between devices, per_device(): lax.psum_scatter(partial_sum, 'wt', scatter_dimension=0, tiled=True)  90.1 us
    all_gather x1, waiting for transfers between devices, per_device(): whole = lax.all_gather(mid, 'wt', axis=1, tiled=True)  87.3 us
    scatter-add x1, other arithmetic, per_device(): jax.ops.segment_sum(parts, down_index.reshape(-1), num_segments=width //...  73.8 us
    all_gather x1, waiting for transfers between devices, carried_in(): gathered = lax.all_gather(x.astype(jnp.bfloat16), axis)  41.4 us
    dot_general x1, matrix products, per_device(): jnp.einsum('lrd,rkde->rkle', act, down_blocks, preferred_element_type=jnp...  21.8 us
    reshape x1, local copies, waits for them, and re-layouts, per_device(): tiles = normed.reshape(rows, width // BLK, BLK)  12 us
    gather x1, local copies, waits for them, and re-layouts, per_device(): picks = jnp.take(tiles, up_index.reshape(-1), axis=1)  11.8 us
    convert_element_type x1, other arithmetic, per_device(): partial_sum = summed.astype(jnp.bfloat16)  9.25 us
  transfers between devices with their start and end apart: 3, of which 3 were waited for; matrix products, arithmetic and copies ran while one was open for 0% of the time, Pallas kernels for 0%

commit v1 on v0

--- a/solution.py
+++ b/solution.py
@@ -59,7 +59,12 @@
     attn = normal_raw.reshape(rows, local_cols) * attn_gain
     mid = (stream.astype(jnp.float32) + attn).astype(jnp.bfloat16)
     width = mlp_gain.shape[0]
-    whole = lax.all_gather(mid, "wt", axis=1, tiled=True)
+    ring = [mid]
+    for hop in range(15):
+        ring.append(lax.ppermute(ring[-1], "wt", [(dev, (dev + 1) % 16) for dev in range(16)]))
+    whole = jnp.roll(
+        jnp.concatenate(ring[::-1], axis=1), (lax.axis_index("wt") + 1) * ring[0].shape[1], axis=1
+    )
     whole_f = whole.astype(jnp.float32)
     scale = lax.rsqrt(jnp.mean(whole_f * whole_f, axis=-1, keepdims=True) + 1e-06)
     normed = (whole_f * scale * mlp_gain).astype(jnp.bfloat16)

time: 393 us -> 556 us (1.41)
  waiting for transfers between devices: 219 us -> 365 us
  local copies, waits for them, and re-layouts: 35.1 us -> 52.8 us
    ppermute x0 -> x15, waiting for transfers between devices: none -> 212 us  [per_device(): lax.ppermute(ring[-1], 'wt', [(dev, (dev + 1) % 16) for dev in range(16)])]
    all_gather x1 -> x0, waiting for transfers between devices: 87.3 us -> none  [per_device(): whole = lax.all_gather(mid, 'wt', axis=1, tiled=True)]
    reduce_scatter x1, waiting for transfers between devices: 90.1 us -> 111 us  [per_device(): lax.psum_scatter(partial_sum, 'wt', scatter_dimension=0, tiled=True)]
    unnamed x19 -> x72, local copies, waits for them, and re-layouts: 1.74 us -> 19.5 us
  transfers between devices with their start and end apart: 3 -> 17, of which waited for: 3 -> 17; matrix products, arithmetic and copies ran while one was open for 0% -> 0% of each run, Pallas kernels for 0% -> 0%
where the time goes in v1:
time: 556 us; the launch traced here: 554 us
  waiting for transfers between devices  365 us (66%)
  other arithmetic  92.3 us (17%)
  local copies, waits for them, and re-layouts  52.8 us (9%)
  matrix products  28.6 us (5%)
  between operations  13.9 us (2%)
    ppermute x15, waiting for transfers between devices, per_device(): lax.ppermute(ring[-1], 'wt', [(dev, (dev + 1) % 16) for dev in range(16)])  212 us
    reduce_scatter x1, waiting for transfers between devices, per_device(): lax.psum_scatter(partial_sum, 'wt', scatter_dimension=0, tiled=True)  111 us
    scatter-add x1, other arithmetic, per_device(): jax.ops.segment_sum(parts, down_index.reshape(-1), num_segments=width //...  73.6 us
    all_gather x1, waiting for transfers between devices, carried_in(): gathered = lax.all_gather(x.astype(jnp.bfloat16), axis)  41.4 us
    dot_general x1, matrix products, per_device(): jnp.einsum('lrd,rkde->rkle', act, down_blocks, preferred_element_type=jnp...  21.8 us
    unnamed x72, local copies, waits for them, and re-layouts  19.5 us
    reshape x1, local copies, waits for them, and re-layouts, per_device(): tiles = normed.reshape(rows, width // BLK, BLK)  12 us
    gather x1, local copies, waits for them, and re-layouts, per_device(): picks = jnp.take(tiles, up_index.reshape(-1), axis=1)  11.8 us
  transfers between devices with their start and end apart: 17, of which 17 were waited for; matrix products, arithmetic and copies ran while one was open for 0% of the time, Pallas kernels for 0%

profile of v1, /device:TPU:2, one launch (start us, length us, event | category | flops | bytes accessed | tf_op | source)
XLA Modules:
  0.0 554.1 jit_solution(6549811507403211026)
XLA Ops:
  6.6 1.6 fusion.27
  8.4 0.9 convolution_convert_fusion
  9.4 1.3 copy.35
  10.7 41.4 %all-gather.3.cloned.1.call-done = bf16[64,128,128]{2,1,0:T(8,128)(2,1)} async-done(((bf16[4,128,128]{2,1,0:T(8,128)(2,1)}), bf16[64,128,128]{2,1,0:T(8,128)(2,1)}) %all-gather.3.cloned.1.call-update) | async-done | bytes 2097168 | tf_op jit(solution)/shard_map/all_gather | solution.py:12
  52.2 3.0 convolution_bitcast_fusion
  55.2 2.8 multiply_reduce_fusion
  58.4 1.6 collective-permute-start
  60.0 15.2 %collective-permute-done = bf16[512,512]{0,1:T(8,128)(2,1)S(1)} collective-permute-done((bf16[512,512]{0,1:T(8,128)(2,1)S(1)}, bf16[512,512]{0,1:T(8,128)(2,1)S(1)}, u32[]{:S(2)}, u32[]{:S(2)}) %collective-permute-start) | collective-permute-done | bytes 524320 | tf_op jit(solution)/shard_map/ppermute | solution.py:64
  75.2 16.1 %collective-permute-done.1 = bf16[512,512]{0,1:T(8,128)(2,1)S(1)} collective-permute-done((bf16[512,512]{0,1:T(8,128)(2,1)S(1)}, bf16[512,512]{0,1:T(8,128)(2,1)S(1)}, u32[]{:S(2)}, u32[]{:S(2)}) %collective-permute-start.1) | collective-permute-done | bytes 524320 | tf_op jit(solution)/shard_map/ppermute | solution.py:64
  91.2 15.2 %collective-permute-done.2 = bf16[512,512]{0,1:T(8,128)(2,1)S(1)} collective-permute-done((bf16[512,512]{0,1:T(8,128)(2,1)S(1)}, bf16[512,512]{0,1:T(8,128)(2,1)S(1)}, u32[]{:S(2)}, u32[]{:S(2)}) %collective-permute-start.2) | collective-permute-done | bytes 524320 | tf_op jit(solution)/shard_map/ppermute | solution.py:64
  106.4 14.3 %collective-permute-done.3 = bf16[512,512]{0,1:T(8,128)(2,1)S(1)} collective-permute-done((bf16[512,512]{0,1:T(8,128)(2,1)S(1)}, bf16[512,512]{0,1:T(8,128)(2,1)S(1)}, u32[]{:S(2)}, u32[]{:S(2)}) %collective-permute-start.3) | collective-permute-done | bytes 524320 | tf_op jit(solution)/shard_map/ppermute | solution.py:64
  120.7 13.4 %collective-permute-done.4 = bf16[512,512]{0,1:T(8,128)(2,1)S(1)} collective-permute-done((bf16[512,512]{0,1:T(8,128)(2,1)S(1)}, bf16[512,512]{0,1:T(8,128)(2,1)S(1)}, u32[]{:S(2)}, u32[]{:S(2)}) %collective-permute-start.4) | collective-permute-done | bytes 524320 | tf_op jit(solution)/shard_map/ppermute | solution.py:64
  134.1 12.5 %collective-permute-done.5 = bf16[512,512]{0,1:T(8,128)(2,1)S(1)} collective-permute-done((bf16[512,512]{0,1:T(8,128)(2,1)S(1)}, bf16[512,512]{0,1:T(8,128)(2,1)S(1)}, u32[]{:S(2)}, u32[]{:S(2)}) %collective-permute-start.5) | collective-permute-done | bytes 524320 | tf_op jit(solution)/shard_map/ppermute | solution.py:64
  146.6 0.8 copy-done.2
  147.4 11.5 %collective-permute-done.6 = bf16[512,512]{0,1:T(8,128)(2,1)S(1)} collective-permute-done((bf16[512,512]{0,1:T(8,128)(2,1)S(1)}, bf16[512,512]{0,1:T(8,128)(2,1)S(1)}, u32[]{:S(2)}, u32[]{:S(2)}) %collective-permute-start.6) | collective-permute-done | bytes 524320 | tf_op jit(solution)/shard_map/ppermute | solution.py:64
  158.9 0.8 copy-done.4
  159.7 12.2 %collective-permute-done.7 = bf16[512,512]{0,1:T(8,128)(2,1)S(1)} collective-permute-done((bf16[512,512]{0,1:T(8,128)(2,1)S(1)}, bf16[512,512]{0,1:T(8,128)(2,1)S(1)}, u32[]{:S(2)}, u32[]{:S(2)}) %collective-permute-start.7) | collective-permute-done | bytes 524320 | tf_op jit(solution)/shard_map/ppermute | solution.py:64
  171.9 0.8 copy-done.6
  172.7 13.3 %collective-permute-done.8 = bf16[512,512]{0,1:T(8,128)(2,1)S(1)} collective-permute-done((bf16[512,512]{0,1:T(8,128)(2,1)S(1)}, bf16[512,512]{0,1:T(8,128)(2,1)S(1)}, u32[]{:S(2)}, u32[]{:S(2)}) %collective-permute-start.8) | collective-permute-done | bytes 524320 | tf_op jit(solution)/shard_map/ppermute | solution.py:64
  186.8 14.3 %collective-permute-done.9 = bf16[512,512]{0,1:T(8,128)(2,1)S(1)} collective-permute-done((bf16[512,512]{0,1:T(8,128)(2,1)S(1)}, bf16[512,512]{0,1:T(8,128)(2,1)S(1)}, u32[]{:S(2)}, u32[]{:S(2)}) %collective-permute-start.9) | collective-permute-done | bytes 524320 | tf_op jit(solution)/shard_map/ppermute | solution.py:64
  201.2 0.8 copy-done.10
  202.0 15.5 %collective-permute-done.10 = bf16[512,512]{0,1:T(8,128)(2,1)S(1)} collective-permute-done((bf16[512,512]{0,1:T(8,128)(2,1)S(1)}, bf16[512,512]{0,1:T(8,128)(2,1)S(1)}, u32[]{:S(2)}, u32[]{:S(2)}) %collective-permute-start.10) | collective-permute-done | bytes 524320 | tf_op jit(solution)/shard_map/ppermute | solution.py:64
  218.2 16.6 %collective-permute-done.11 = bf16[512,512]{0,1:T(8,128)(2,1)S(1)} collective-permute-done((bf16[512,512]{0,1:T(8,128)(2,1)S(1)}, bf16[512,512]{0,1:T(8,128)(2,1)S(1)}, u32[]{:S(2)}, u32[]{:S(2)}) %collective-permute-start.11) | collective-permute-done | bytes 524320 | tf_op jit(solution)/shard_map/ppermute | solution.py:64
  235.6 15.7 %collective-permute-done.12 = bf16[512,512]{0,1:T(8,128)(2,1)} collective-permute-done((bf16[512,512]{0,1:T(8,128)(2,1)S(1)}, bf16[512,512]{0,1:T(8,128)(2,1)}, u32[]{:S(2)}, u32[]{:S(2)}) %collective-permute-start.12) | collective-permute-done | bytes 524320 | tf_op jit(solution)/shard_map/ppermute | solution.py:64
  251.5 14.8 %collective-permute-done.13 = bf16[512,512]{0,1:T(8,128)(2,1)} collective-permute-done((bf16[512,512]{0,1:T(8,128)(2,1)}, bf16[512,512]{0,1:T(8,128)(2,1)}, u32[]{:S(2)}, u32[]{:S(2)}) %collective-permute-start.13) | collective-permute-done | bytes 524320 | tf_op jit(solution)/shard_map/ppermute | solution.py:64
  266.3 11.5 %collective-permute-done.14 = bf16[512,512]{0,1:T(8,128)(2,1)S(1)} collective-permute-done((bf16[512,512]{0,1:T(8,128)(2,1)}, bf16[512,512]{0,1:T(8,128)(2,1)S(1)}, u32[]{:S(2)}, u32[]{:S(2)}) %collective-permute-start.14) | collective-permute-done | bytes 524320 | tf_op jit(solution)/shard_map/ppermute | solution.py:64
  277.8 1.1 constant_dynamic-update-slice_fusion.30
  278.9 1.1 constant_dynamic-update-slice_fusion.29
  280.0 1.1 constant_dynamic-update-slice_fusion.28
  281.1 1.1 constant_dynamic-update-slice_fusion.27
  282.2 1.1 constant_dynamic-update-slice_fusion.26
  283.3 1.1 constant_dynamic-update-slice_fusion.25
  284.3 1.1 constant_dynamic-update-slice_fusion.24
  285.4 1.1 constant_dynamic-update-slice_fusion.23
  286.5 1.1 constant_dynamic-update-slice_fusion.22
  287.9 1.1 constant_dynamic-update-slice_fusion.14
  289.0 1.1 constant_dynamic-update-slice_fusion.13
  290.7 1.8 fusion
  292.5 4.4 fusion.2
  296.9 12.0 %copy.43 = bf16[512,64,128]{2,0,1:T(8,128)(2,1)} copy(bf16[512,64,128]{0,2,1:T(8,128)(2,1)} %bitcast.96) | data formatting | bytes 16777216 | tf_op jit(solution)/shard_map/reshape | solution.py:71
  308.9 11.8 %gather_fusion = bf16[128,512,128]{2,1,0:T(8,128)(2,1)} fusion(bf16[512,64,128]{2,0,1:T(8,128)(2,1)} %copy.43, s32[1024]{0:T(1024)S(1)} %pad_clamp_fusion), kind=kCustom, calls=%fused_computation | custom fusion | bytes 33554944 | tf_op jit(solution)/shard_map/jit(_take)/gather | solution.py:73
  320.7 21.8 %fusion.20 = f32[8,512,16,128]{3,1,2,0:T(8,128)} fusion(bf16[8,16,128,128]{3,2,1,0:T(8,128)(2,1)} %param.21, bf16[8,16,128,128]{3,2,1,0:T(8,128)(2,1)} %param.19, bf16[512,8,16,128]{3,0,2,1:T(8,128)(2,1)} %bitcast.95, pred[8,16]{1,0:T(8,128)(4,1)S(1)} %compare_and_fusion), kind=kOutput, calls=%fused_computation.28 | convolution fusion | flops 4305977344 | bytes 58720384 | tf_op jit(solution)/shard_map/lrd,rkde->rkle/dot_general | solution.py:77
  342.5 7.8 %broadcast_in_dim.43 = f32[64,512,128]{2,1,0:T(8,128)} broadcast(f32[]{:T(128)} %constant.67.clone.1), dimensions={} | broadcast | bytes 16777220 | tf_op jit(solution)/shard_map/broadcast_in_dim | solution.py:79
  350.3 73.6 %scatter_fusion = f32[64,512,128]{2,1,0:T(8,128)} fusion(f32[64,512,128]{2,1,0:T(8,128)} %broadcast_in_dim.43, s32[128]{0:T(128)S(1)} %reshape.114, f32[128,512,128]{2,1,0:T(8,128)} %bitcast.94), kind=kCustom, calls=%fused_computation.1 | custom fusion | flops 8388608 | bytes 100663808 | tf_op jit(solution)/shard_map/scatter-add | solution.py:79
  423.9 9.2 %convert_element_type.62 = bf16[64,512,128]{2,1,0:T(8,128)(2,1)} convert(f32[64,512,128]{2,1,0:T(8,128)} %scatter_fusion) | non-fusion elementwise | flops 4194304 | bytes 25165824 | tf_op jit(solution)/shard_map/convert_element_type | solution.py:80
  433.2 111.4 %reduce-scatter.2.cloned.1.call-done = bf16[4,512,128]{2,1,0:T(8,128)(2,1)} async-done(((bf16[64,512,128]{2,1,0:T(8,128)(2,1)}), bf16[4,512,128]{2,1,0:T(8,128)(2,1)}) %reduce-scatter.2.cloned.1.call-update) | async-done | bytes 524304 | tf_op jit(solution)/shard_map/reduce_scatter | solution.py:81
  544.6 1.1 convert_bitcast_fusion
  546.2 1.0 copy.45
  (90 shorter events, 4.7 us)
Async XLA Ops:
  6.5 1.8 copy-start
  6.5 51.7 %copy-start.19 = (f32[512]{0:T(512)S(1)}, f32[512]{0:T(512)}, u32[]{:S(2)}) copy-start(f32[512]{0:T(512)} %param.16) | copy-start | bytes 6148
  6.5 244.8 %copy-start.18 = (s32[8,16]{1,0:T(8,128)S(1)}, s32[8,16]{1,0:T(8,128)}, u32[]{:S(2)}) copy-start(s32[8,16]{1,0:T(8,128)} %param.20) | copy-start | bytes 1540
  6.5 244.8 %copy-start.17 = (s32[8,16]{1,0:T(8,128)S(1)}, s32[8,16]{1,0:T(8,128)}, u32[]{:S(2)}) copy-start(s32[8,16]{1,0:T(8,128)} %param.18) | copy-start | bytes 1540
  6.5 45.6 %all-gather.3.cloned.1.call-start = ((), (), s32[]{:S(2)}) async-start(), calls=%async_computation.2 | async-start | bytes 2228224 | tf_op jit(solution)/shard_map/all_gather | solution.py:12
  9.3 535.3 %reduce-scatter.2.cloned.1.call-start = ((), (), s32[]{:S(2)}) async-start(), calls=%async_computation.1 | async-start | bytes 8912896 | tf_op jit(solution)/shard_map/reduce_scatter | solution.py:81
  58.4 16.7 %collective-permute-start = (bf16[512,512]{0,1:T(8,128)(2,1)S(1)}, bf16[512,512]{0,1:T(8,128)(2,1)S(1)}, u32[]{:S(2)}, u32[]{:S(2)}) collective-permute-start(bf16[512,512]{0,1:T(8,128)(2,1)S(1)} %fusion.30), channel_id=1, source_target_pairs={{0,1},{1,2},{2,3},{3,4},{4,5},{5,6},{6,7},{7,8},{8,9},{9,10},{10,1... | collective-permute-start | bytes 1572872 | tf_op jit(solution)/shard_map/ppermute | solution.py:64
  75.2 16.1 %collective-permute-start.1 = (bf16[512,512]{0,1:T(8,128)(2,1)S(1)}, bf16[512,512]{0,1:T(8,128)(2,1)S(1)}, u32[]{:S(2)}, u32[]{:S(2)}) collective-permute-start(bf16[512,512]{0,1:T(8,128)(2,1)S(1)} %collective-permute-done), channel_id=1, source_target_pairs={{0,1},{1,2},{2,3},{3,4},{4,5},{5,6},{6,7},{7,8},{8,9},{9,10},{10,1... | collective-permute-start | bytes 1572872 | tf_op jit(solution)/shard_map/ppermute | solution.py:64
  91.2 15.2 %collective-permute-start.2 = (bf16[512,512]{0,1:T(8,128)(2,1)S(1)}, bf16[512,512]{0,1:T(8,128)(2,1)S(1)}, u32[]{:S(2)}, u32[]{:S(2)}) collective-permute-start(bf16[512,512]{0,1:T(8,128)(2,1)S(1)} %collective-permute-done.1), channel_id=1, source_target_pairs={{0,1},{1,2},{2,3},{3,4},{4,5},{5,6},{6,7},{7,8},{8,9},{9,10},{10,1... | collective-permute-start | bytes 1572872 | tf_op jit(solution)/shard_map/ppermute | solution.py:64
  106.4 14.3 %collective-permute-start.3 = (bf16[512,512]{0,1:T(8,128)(2,1)S(1)}, bf16[512,512]{0,1:T(8,128)(2,1)S(1)}, u32[]{:S(2)}, u32[]{:S(2)}) collective-permute-start(bf16[512,512]{0,1:T(8,128)(2,1)S(1)} %collective-permute-done.2), channel_id=1, source_target_pairs={{0,1},{1,2},{2,3},{3,4},{4,5},{5,6},{6,7},{7,8},{8,9},{9,10},{10,1... | collective-permute-start | bytes 1572872 | tf_op jit(solution)/shard_map/ppermute | solution.py:64
  120.7 13.4 %collective-permute-start.4 = (bf16[512,512]{0,1:T(8,128)(2,1)S(1)}, bf16[512,512]{0,1:T(8,128)(2,1)S(1)}, u32[]{:S(2)}, u32[]{:S(2)}) collective-permute-start(bf16[512,512]{0,1:T(8,128)(2,1)S(1)} %collective-permute-done.3), channel_id=1, source_target_pairs={{0,1},{1,2},{2,3},{3,4},{4,5},{5,6},{6,7},{7,8},{8,9},{9,10},{10,1... | collective-permute-start | bytes 1572872 | tf_op jit(solution)/shard_map/ppermute | solution.py:64
  134.1 12.5 %collective-permute-start.5 = (bf16[512,512]{0,1:T(8,128)(2,1)S(1)}, bf16[512,512]{0,1:T(8,128)(2,1)S(1)}, u32[]{:S(2)}, u32[]{:S(2)}) collective-permute-start(bf16[512,512]{0,1:T(8,128)(2,1)S(1)} %collective-permute-done.4), channel_id=1, source_target_pairs={{0,1},{1,2},{2,3},{3,4},{4,5},{5,6},{6,7},{7,8},{8,9},{9,10},{10,1... | collective-permute-start | bytes 1572872 | tf_op jit(solution)/shard_map/ppermute | solution.py:64
  146.6 0.8 copy-start.2
  147.4 11.5 %collective-permute-start.6 = (bf16[512,512]{0,1:T(8,128)(2,1)S(1)}, bf16[512,512]{0,1:T(8,128)(2,1)S(1)}, u32[]{:S(2)}, u32[]{:S(2)}) collective-permute-start(bf16[512,512]{0,1:T(8,128)(2,1)S(1)} %collective-permute-done.5), channel_id=1, source_target_pairs={{0,1},{1,2},{2,3},{3,4},{4,5},{5,6},{6,7},{7,8},{8,9},{9,10},{10,1... | collective-permute-start | bytes 1572872 | tf_op jit(solution)/shard_map/ppermute | solution.py:64
  158.9 0.8 copy-start.4
  159.7 12.2 %collective-permute-start.7 = (bf16[512,512]{0,1:T(8,128)(2,1)S(1)}, bf16[512,512]{0,1:T(8,128)(2,1)S(1)}, u32[]{:S(2)}, u32[]{:S(2)}) collective-permute-start(bf16[512,512]{0,1:T(8,128)(2,1)S(1)} %collective-permute-done.6), channel_id=1, source_target_pairs={{0,1},{1,2},{2,3},{3,4},{4,5},{5,6},{6,7},{7,8},{8,9},{9,10},{10,1... | collective-permute-start | bytes 1572872 | tf_op jit(solution)/shard_map/ppermute | solution.py:64
  171.9 0.8 copy-start.6
  172.7 13.3 %collective-permute-start.8 = (bf16[512,512]{0,1:T(8,128)(2,1)S(1)}, bf16[512,512]{0,1:T(8,128)(2,1)S(1)}, u32[]{:S(2)}, u32[]{:S(2)}) collective-permute-start(bf16[512,512]{0,1:T(8,128)(2,1)S(1)} %collective-permute-done.7), channel_id=1, source_target_pairs={{0,1},{1,2},{2,3},{3,4},{4,5},{5,6},{6,7},{7,8},{8,9},{9,10},{10,1... | collective-permute-start | bytes 1572872 | tf_op jit(solution)/shard_map/ppermute | solution.py:64
  186.0 0.8 copy-start.8
  186.8 14.3 %collective-permute-start.9 = (bf16[512,512]{0,1:T(8,128)(2,1)S(1)}, bf16[512,512]{0,1:T(8,128)(2,1)S(1)}, u32[]{:S(2)}, u32[]{:S(2)}) collective-permute-start(bf16[512,512]{0,1:T(8,128)(2,1)S(1)} %collective-permute-done.8), channel_id=1, source_target_pairs={{0,1},{1,2},{2,3},{3,4},{4,5},{5,6},{6,7},{7,8},{8,9},{9,10},{10,1... | collective-permute-start | bytes 1572872 | tf_op jit(solution)/shard_map/ppermute | solution.py:64
  201.2 0.8 copy-start.10
  202.0 15.5 %collective-permute-start.10 = (bf16[512,512]{0,1:T(8,128)(2,1)S(1)}, bf16[512,512]{0,1:T(8,128)(2,1)S(1)}, u32[]{:S(2)}, u32[]{:S(2)}) collective-permute-start(bf16[512,512]{0,1:T(8,128)(2,1)S(1)} %collective-permute-done.9), channel_id=1, source_target_pairs={{0,1},{1,2},{2,3},{3,4},{4,5},{5,6},{6,7},{7,8},{8,9},{9,10},{10,1... | collective-permute-start | bytes 1572872 | tf_op jit(solution)/shard_map/ppermute | solution.py:64
  217.4 0.8 copy-start.12
  218.2 16.6 %collective-permute-start.11 = (bf16[512,512]{0,1:T(8,128)(2,1)S(1)}, bf16[512,512]{0,1:T(8,128)(2,1)S(1)}, u32[]{:S(2)}, u32[]{:S(2)}) collective-permute-start(bf16[512,512]{0,1:T(8,128)(2,1)S(1)} %collective-permute-done.10), channel_id=1, source_target_pairs={{0,1},{1,2},{2,3},{3,4},{4,5},{5,6},{6,7},{7,8},{8,9},{9,10},{10,1... | collective-permute-start | bytes 1572872 | tf_op jit(solution)/shard_map/ppermute | solution.py:64
  234.8 0.8 copy-start.14
  235.6 15.7 %collective-permute-start.12 = (bf16[512,512]{0,1:T(8,128)(2,1)S(1)}, bf16[512,512]{0,1:T(8,128)(2,1)}, u32[]{:S(2)}, u32[]{:S(2)}) collective-permute-start(bf16[512,512]{0,1:T(8,128)(2,1)S(1)} %collective-permute-done.11), channel_id=1, source_target_pairs={{0,1},{1,2},{2,3},{3,4},{4,5},{5,6},{6,7},{7,8},{8,9},{9,10},{10,1... | collective-permute-start | bytes 1572872 | tf_op jit(solution)/shard_map/ppermute | solution.py:64
  251.3 15.0 %collective-permute-start.13 = (bf16[512,512]{0,1:T(8,128)(2,1)}, bf16[512,512]{0,1:T(8,128)(2,1)}, u32[]{:S(2)}, u32[]{:S(2)}) collective-permute-start(bf16[512,512]{0,1:T(8,128)(2,1)} %collective-permute-done.12), channel_id=1, source_target_pairs={{0,1},{1,2},{2,3},{3,4},{4,5},{5,6},{6,7},{7,8},{8,9},{9,10},{10,1... | collective-permute-start | bytes 1572872 | tf_op jit(solution)/shard_map/ppermute | solution.py:64
  251.5 38.6 %copy-start.15 = (bf16[512,512]{0,1:T(8,128)(2,1)S(1)}, bf16[512,512]{0,1:T(8,128)(2,1)}, u32[]{:S(2)}) copy-start(bf16[512,512]{0,1:T(8,128)(2,1)} %copy-done.14) | copy-start | bytes 1572868
  251.5 38.7 %copy-start.13 = (bf16[512,512]{0,1:T(8,128)(2,1)S(1)}, bf16[512,512]{0,1:T(8,128)(2,1)}, u32[]{:S(2)}) copy-start(bf16[512,512]{0,1:T(8,128)(2,1)} %copy-done.12) | copy-start | bytes 1572868
  251.5 38.7 %copy-start.11 = (bf16[512,512]{0,1:T(8,128)(2,1)S(1)}, bf16[512,512]{0,1:T(8,128)(2,1)}, u32[]{:S(2)}) copy-start(bf16[512,512]{0,1:T(8,128)(2,1)} %copy-done.10) | copy-start | bytes 1572868
  251.5 38.7 %copy-start.9 = (bf16[512,512]{0,1:T(8,128)(2,1)S(1)}, bf16[512,512]{0,1:T(8,128)(2,1)}, u32[]{:S(2)}) copy-start(bf16[512,512]{0,1:T(8,128)(2,1)} %copy-done.8) | copy-start | bytes 1572868
  251.5 38.8 %copy-start.7 = (bf16[512,512]{0,1:T(8,128)(2,1)S(1)}, bf16[512,512]{0,1:T(8,128)(2,1)}, u32[]{:S(2)}) copy-start(bf16[512,512]{0,1:T(8,128)(2,1)} %copy-done.6) | copy-start | bytes 1572868
  251.5 38.8 %copy-start.5 = (bf16[512,512]{0,1:T(8,128)(2,1)S(1)}, bf16[512,512]{0,1:T(8,128)(2,1)}, u32[]{:S(2)}) copy-start(bf16[512,512]{0,1:T(8,128)(2,1)} %copy-done.4) | copy-start | bytes 1572868
  251.5 38.9 %copy-start.3 = (bf16[512,512]{0,1:T(8,128)(2,1)S(1)}, bf16[512,512]{0,1:T(8,128)(2,1)}, u32[]{:S(2)}) copy-start(bf16[512,512]{0,1:T(8,128)(2,1)} %copy-done.2) | copy-start | bytes 1572868
  266.3 11.5 %collective-permute-start.14 = (bf16[512,512]{0,1:T(8,128)(2,1)}, bf16[512,512]{0,1:T(8,128)(2,1)S(1)}, u32[]{:S(2)}, u32[]{:S(2)}) collective-permute-start(bf16[512,512]{0,1:T(8,128)(2,1)} %collective-permute-done.13), channel_id=1, source_target_pairs={{0,1},{1,2},{2,3},{3,4},{4,5},{5,6},{6,7},{7,8},{8,9},{9,10},{10,1... | collective-permute-start | bytes 1572872 | tf_op jit(solution)/shard_map/ppermute | solution.py:64
  285.4 7.1 %copy-start.16 = (f32[8192]{0:T(1024)S(1)}, f32[8192]{0:T(1024)}, u32[]{:S(2)}) copy-start(f32[8192]{0:T(1024)} %param.17) | copy-start | bytes 98308
  350.3 196.9 %copy-start.1 = (bf16[512,512]{1,0:T(8,128)(2,1)S(1)}, bf16[512,512]{1,0:T(8,128)(2,1)}, u32[]{:S(2)}) copy-start(bf16[512,512]{1,0:T(8,128)(2,1)} %param.14) | copy-start | bytes 1572868
Sparse Core Ops, SparseCore 0:
  9.5 42.6 all-gather.2
  433.3 111.2 reduce-scatter.1
